TPU v7x, 256 devices: a whole 4x4x8 slice. The times are simulated.
256 devices in a mesh: row: 32 (over y, x, core), col: 8 (over z).
Axes of the slice: x: 4, y: 4, z: 8, core: 2. Of those that a mesh axis runs over, the one named last changes fastest.
Arguments:
- points: bfloat16 [32, 98304], P(None, ('row', 'col')), may hold values from -2.6875 to 2.6875
- solution: float32 [4, 98304], P(None, ('row', 'col')), may hold values from -6 to 6
- residual: float32 [4, 98304], P(None, ('row', 'col')), may hold values from -8 to 8
- direction: float32 [4, 98304], P(None, ('row', 'col')), may hold values from -8 to 8
- outscale: float32 [4], replicated, may hold values from 0.5 to 2
- noise_var: float32 [4], replicated, may hold values from 0.05 to 0.5
Outputs:
- solution_new: float32 [4, 98304], P(None, ('row', 'col'))
- residual_new: float32 [4, 98304], P(None, ('row', 'col'))
- direction_new: float32 [4, 98304], P(None, ('row', 'col'))
All inputs are finite; a program needn't handle non-finite values.
Results may differ from a plain program's by a relative error of at most 0.0007.
Values may be sent and summed in bfloat16 or wider, within the bound.
No kernel may reach another device: no remote copies, remote signals or barrier semaphores. Data moves between devices by JAX's collectives and lax.ppermute only.
A program may use at most 64 MiB of HBM per device.

v0:
```python
import functools
import math

import jax
import jax.numpy as jnp
from jax import lax
from jax.experimental import pallas as pl
from jax.experimental.pallas import tpu as pltpu
from jax.sharding import Mesh
from jax.sharding import PartitionSpec as P

SIZES = (4, 4, 2, 8)
AXES = ("y", "x", "core", "z")
GROUP = ("y", "core")
IN, OBJ, WIDTH = 32, 4, 384
BLOCKS = 8
LANES = BLOCKS * WIDTH
HALF = LANES // 2
DEPTH = 128
PACK = 48
LOG2E = 1.0 / math.log(2.0)
SCALE = 5.0 / 9.0
VMEM = pl.BlockSpec(memory_space=pltpu.VMEM)
SMEM = pl.BlockSpec(memory_space=pltpu.SMEM)


def params(mebibytes=48):
    return pltpu.CompilerParams(vmem_limit_bytes=mebibytes * 1024 * 1024)


def parts(x, count):
    out = []
    for _ in range(count):
        out.append(x.astype(jnp.bfloat16).astype(jnp.float32))
        x = x - out[-1]
    return out


def rows_of(values, shape):
    where = lax.broadcasted_iota(jnp.int32, shape, 0)
    out = jnp.zeros(shape, jnp.float32)
    for i, value in enumerate(values):
        out = jnp.where(where == i, value, out)
    return out


def row_features(pts):
    wide = pts.astype(jnp.float32)
    own = SCALE * jnp.sum(wide * wide, axis=0, keepdims=True)
    extra = rows_of([1.0] * 3 + parts(own, 3), (16, WIDTH))
    zeros = jnp.zeros((16, WIDTH), jnp.float32)
    whole = jnp.concatenate(parts((-2.0 * SCALE) * wide, 3) + [extra, zeros], axis=0)
    return whole.astype(jnp.bfloat16)


def col_features(pts):
    wide = pts.astype(jnp.float32)
    own = SCALE * jnp.sum(wide * wide, axis=0, keepdims=True)
    extra = rows_of(parts(own, 3) + [1.0] * 3, (16, WIDTH))
    zeros = jnp.zeros((16, WIDTH), jnp.float32)
    whole = jnp.concatenate([wide, wide, wide, extra, zeros], axis=0)
    return whole.T.astype(jnp.bfloat16)


def dot(a, b, dims=((1,), (0,))):
    return lax.dot_general(a, b, (dims, ((), ())), preferred_element_type=jnp.float32)


def weights(sq):
    sq = jnp.maximum(sq, 1e-30)
    v = sq * lax.rsqrt(sq)
    w = ((sq + v) + 1.0 / 3.0) * jnp.exp2(v * (-3.0 * LOG2E))
    hi = w.astype(jnp.bfloat16)
    lo = ((w - hi.astype(jnp.float32)) * LOW).astype(FINE)
    return hi, lo


def both(a, hi, lo, dims=((1,), (0,))):
    return dot(a[0], hi, dims) + (1.0 / LOW) * dot(a[1], lo, dims)


def fine(tail):
    wide = folded(tail.astype(jnp.float32))
    high = wide.astype(FINE).astype(jnp.float32)
    zeros = jnp.zeros((16 - 2 * OBJ, wide.shape[1]), jnp.float32)
    return jnp.concatenate([high, wide - high, zeros], axis=0).astype(FINE)


TRANSPOSED = ((1,), (1,))
STRIP = 256
LOW = 2.0**14
FINE = jnp.float8_e4m3fn


def pipeline(count, spare, place_of, bt, ax, dr, dr8, dc, dc8, row_acc, col_acc, stages):
    xa, xb, ha, hb, la, lb = stages

    def distances(step, out, o):
        i, at, _ = place_of(step)
        out[:, o : o + STRIP] = dot(bt[i], ax[:, pl.ds(pl.multiple_of(at + o, 128), STRIP)])

    def by_col(step, hi, lo, o):
        _, _, at = place_of(step)
        lanes = pl.ds(pl.multiple_of(at + o, 128), STRIP)
        return both((dr[:, lanes], dr8[:, lanes]), hi[:, o : o + STRIP], lo[:, o : o + STRIP], TRANSPOSED)

    def by_row(step, hi, lo, o, first):
        i, at, _ = place_of(step)
        lanes = pl.ds(pl.multiple_of(jnp.where(first, LANES, at) + o, 128), STRIP)
        row_acc[:, lanes] += both((dc[i], dc8[i]), hi[:, o : o + STRIP], lo[:, o : o + STRIP])

    def half(step, x, x_next, hi, lo, hi_last, lo_last):
        last, following = jnp.maximum(step - 1, 0), jnp.minimum(step + 1, count - 1)
        total = None
        for o in range(0, HALF, STRIP):
            distances(following, x_next, o)
            part = by_col(last, hi_last, lo_last, o)
            total = part if total is None else total + part
            by_row(last, hi_last, lo_last, o, step == 0)
            got = weights(x[:, o : o + STRIP])
            hi[:, o : o + STRIP], lo[:, o : o + STRIP] = got
        col_acc[jnp.where(step == 0, spare, place_of(last)[0])] += total

    for o in range(0, HALF, STRIP):
        distances(0, xa, o)

    @pl.loop(0, count // 2)
    def _(pair):
        half(2 * pair, xa, xb, ha, la, hb, lb)
        half(2 * pair + 1, xb, xa, hb, lb, ha, la)

    total = None
    for o in range(0, HALF, STRIP):
        part = by_col(count - 1, hb, lb, o)
        total = part if total is None else total + part
        by_row(count - 1, hb, lb, o, False)
    col_acc[place_of(count - 1)[0]] += total


def stages():
    block = (WIDTH, HALF)
    return [pltpu.VMEM(block, jnp.float32)] * 2 + [pltpu.VMEM(block, jnp.bfloat16)] * 2 + [pltpu.VMEM(block, FINE)] * 2


def folded(x):
    return x[:OBJ] + x[OBJ : 2 * OBJ]


def pack_kernel(points, direction, residual, solution, outscale, noise, out, own, kept):
    wide = direction[...]
    high, low = parts(wide, 2)
    tail = jnp.concatenate([high, low, jnp.zeros((8, WIDTH), jnp.float32)], axis=0)
    tail = tail.astype(jnp.bfloat16)
    own[0, :IN, :] = points[...]
    own[0, IN:, :] = tail
    for i in range(BLOCKS):
        out[i, :IN, :] = points[...]
        out[i, IN:, :] = tail
    kept[0] = wide
    kept[1] = residual[...]
    kept[2] = solution[...]
    for o in range(OBJ):
        kept[3, o : o + 1, :] = jnp.full((1, WIDTH), 3.0 * outscale[o], jnp.float32)
        kept[4, o : o + 1, :] = jnp.full((1, WIDTH), noise[o], jnp.float32)


def near_kernel(place, r0, r1, r2, r3, cols, ax, dr, dr8, row_out, col_near, row_acc, rows, bt, dc, dc8, col_acc, *work):
    y, core, z = place[0], place[1], place[3]
    h = 2 * y + core
    for k, ref in enumerate((r0, r1, r2, r3)):
        rows[2 * k] = ref[0]
        rows[2 * k + 1] = ref[1]
    for i in range(BLOCKS):
        there = lax.rem(h + i, BLOCKS)
        away = lax.rem(y - there // 2 + 4, 4)
        other = jnp.where(lax.rem(there, 2) == core, 0, 1)
        block = rows[2 * away + other]
        lanes = pl.ds(i * WIDTH, WIDTH)
        ax[:, lanes] = row_features(block[:IN])
        tail = block[IN:]
        tail8 = fine(tail)
        dr[:, lanes], dr8[:, lanes] = tail, tail8
        if i < BLOCKS // 2:
            lanes = pl.ds(LANES + i * WIDTH, WIDTH)
            dr[:, lanes] = jnp.zeros_like(tail) if i == 0 else tail
            dr8[:, lanes] = jnp.zeros_like(tail8) if i == 0 else tail8
    row_acc[...] = jnp.zeros_like(row_acc)
    col_acc[...] = jnp.zeros_like(col_acc)
    for i in range(5):
        block = cols[lax.rem(z + i, BLOCKS)]
        bt[i] = col_features(block[:IN])
        dc[i], dc8[i] = block[IN:], fine(block[IN:])
    tie = jnp.where(z < BLOCKS // 2, 0, WIDTH)

    def place_of(s):
        i = jnp.where(s < 6, 1 + s // 2, jnp.where(s == 6, 4, 0))
        at = jnp.where(s < 6, lax.rem(s, 2) * HALF, jnp.where(s == 6, tie, 0))
        return i, at, jnp.where(s == 7, LANES, at)

    pipeline(8, 5, place_of, bt, ax, dr, dr8, dc, dc8, row_acc, col_acc, work)

    lanes = pl.ds(HALF, WIDTH)
    hi, lo = weights(dot(bt[0], ax[:, lanes]))
    row_acc[:, lanes] += both((dc[0], dc8[0]), hi, lo)
    row_out[...] = row_acc[:, :LANES]
    for i in range(BLOCKS):
        got = folded(col_acc[i]) if i < 5 else jnp.zeros((OBJ, WIDTH), jnp.float32)
        col_near[lax.rem(z + i, BLOCKS)] = got


def far_kernel(place, ax, dr, dr8, row_in, cols1, cols2, row_out, col1, col2, row_acc, bt, dc, dc8, col_acc, *work):
    y, core, x, z = place[0], place[1], place[2], place[3]
    h = 2 * y + core
    row_acc[:, :LANES] = row_in[...]
    col_acc[...] = jnp.zeros_like(col_acc)
    first = z + jnp.where(x < 2, 0, 1)
    for i in range(12):
        block = cols1[i] if i < BLOCKS else cols2[lax.rem(first + i, BLOCKS)]
        bt[i] = col_features(block[:IN])
        dc[i], dc8[i] = block[IN:], fine(block[IN:])

    def place_of(s):
        at = lax.rem(s, 2) * HALF
        return s // 2, at, at

    pipeline(24, 12, place_of, bt, ax, dr, dr8, dc, dc8, row_acc, col_acc, work)
    for i in range(BLOCKS):
        row_out[lax.rem(h + i, BLOCKS)] = folded(row_acc[:, pl.ds(i * WIDTH, WIDTH)])
        col1[i] = folded(col_acc[i])
        got = folded(col_acc[BLOCKS + i]) if i < 4 else jnp.zeros((OBJ, WIDTH), jnp.float32)
        col2[lax.rem(first + i, BLOCKS)] = got


def join_kernel(near, one, two, out):
    out[...] = near[...] + one[...] + two[...]


def image_kernel(by_rows, by_cols, kept, image, sums):
    total = jnp.zeros((OBJ, WIDTH), jnp.float32)
    for i in range(BLOCKS):
        total = total + by_rows[i] + by_cols[i]
    d, r = kept[0], kept[1]
    got = kept[3] * total + kept[4] * d
    image[...] = got
    products = jnp.concatenate([r * r, d * got, r * got, got * got], axis=0)
    column = jnp.sum(products, axis=1, keepdims=True)
    shape = (4 * OBJ, 128)
    diagonal = lax.broadcasted_iota(jnp.int32, shape, 0) == lax.broadcasted_iota(jnp.int32, shape, 1)
    row = jnp.sum(jnp.where(diagonal, column, 0.0), axis=0, keepdims=True)
    sums[...] = jnp.broadcast_to(row, sums.shape)


def update_kernel(sums, kept, image, solution_new, residual_new, direction_new):
    total = jnp.sum(sums[...], axis=0, keepdims=True)
    lane = lax.broadcasted_iota(jnp.int32, (OBJ, 128), 1) - lax.broadcasted_iota(jnp.int32, (OBJ, 128), 0)

    def kind(k):
        return jnp.sum(jnp.where(lane == k * OBJ, total, 0.0), axis=1, keepdims=True)

    norm_old, curvature, cross, square = kind(0), kind(1), kind(2), kind(3)
    step_len = norm_old / curvature
    norm_new = jnp.maximum(norm_old - 2.0 * step_len * cross + step_len * step_len * square, 0.0)
    ratio_new = norm_new / (norm_old + 1e-06)
    d = kept[0]
    solution_new[...] = kept[2] + step_len * d
    moved = kept[1] - step_len * image[...]
    residual_new[...] = moved
    direction_new[...] = moved + ratio_new * d


def f32(*shape):
    return jax.ShapeDtypeStruct(shape, jnp.float32)


def bf16(*shape):
    return jax.ShapeDtypeStruct(shape, jnp.bfloat16)


def exchanged(x, axis):
    return lax.all_to_all(x, axis, 0, 0)


def from_ahead(x, axis, by):
    length = lax.axis_size(axis)
    return lax.ppermute(x, axis, [(i, (i - by) % length) for i in range(length)])


def shards(points, solution, residual, direction, outscale, noise_var):
    devices = math.prod(SIZES)
    place = jnp.stack([lax.axis_index(a) for a in ("y", "core", "x", "z")]).astype(jnp.int32)
    packed, own, kept = pl.pallas_call(
        pack_kernel,
        in_specs=[VMEM] * 4 + [SMEM] * 2,
        out_specs=[VMEM] * 3,
        out_shape=[bf16(BLOCKS, PACK, WIDTH), bf16(1, PACK, WIDTH), f32(5, OBJ, WIDTH)],
    )(points, direction, residual, solution, outscale, noise_var)
    pair = jnp.concatenate([own, from_ahead(own, "core", 1)], axis=0)
    rows = [pair] + [from_ahead(pair, "y", -k) for k in (1, 2, 3)]
    cols = exchanged(packed, "z")
    cols1, cols2 = from_ahead(cols, "x", 1), from_ahead(cols, "x", 2)
    ax, dr, dr8, row_acc, col_near = pl.pallas_call(
        near_kernel,
        in_specs=[SMEM] + [VMEM] * 5,
        out_specs=[VMEM] * 5,
        out_shape=[
            bf16(DEPTH, LANES),
            bf16(16, LANES + HALF),
            jax.ShapeDtypeStruct((16, LANES + HALF), FINE),
            f32(16, LANES),
            f32(BLOCKS, OBJ, WIDTH),
        ],
        scratch_shapes=[
            pltpu.VMEM((16, LANES + HALF), jnp.float32),
            pltpu.VMEM((BLOCKS, PACK, WIDTH), jnp.bfloat16),
            pltpu.VMEM((5, WIDTH, DEPTH), jnp.bfloat16),
            pltpu.VMEM((5, 16, WIDTH), jnp.bfloat16),
            pltpu.VMEM((5, 16, WIDTH), FINE),
            pltpu.VMEM((6, 16, WIDTH), jnp.float32),
        ]
        + stages(),
        compiler_params=params(),
        cost_estimate=pl.CostEstimate(flops=8 * 10**9, bytes_accessed=10**6, transcendentals=10**7),
    )(place, *rows, cols)
    by_rows, col1, col2 = pl.pallas_call(
        far_kernel,
        in_specs=[SMEM] + [VMEM] * 6,
        out_specs=[VMEM] * 3,
        out_shape=[f32(BLOCKS, OBJ, WIDTH)] * 3,
        scratch_shapes=[
            pltpu.VMEM((16, LANES + HALF), jnp.float32),
            pltpu.VMEM((12, WIDTH, DEPTH), jnp.bfloat16),
            pltpu.VMEM((12, 16, WIDTH), jnp.bfloat16),
            pltpu.VMEM((12, 16, WIDTH), FINE),
            pltpu.VMEM((13, 16, WIDTH), jnp.float32),
        ]
        + stages(),
        compiler_params=params(),
        cost_estimate=pl.CostEstimate(flops=24 * 10**9, bytes_accessed=10**6, transcendentals=10**7),
    )(place, ax, dr, dr8, row_acc, cols1, cols2)
    col1, col2 = from_ahead(col1, "x", -1), from_ahead(col2, "x", -2)
    by_rows = exchanged(by_rows, GROUP)
    by_cols = pl.pallas_call(
        join_kernel,
        in_specs=[VMEM] * 3,
        out_specs=VMEM,
        out_shape=f32(BLOCKS, OBJ, WIDTH),
        compiler_params=params(4),
    )(col_near, col1, col2)
    by_cols = exchanged(by_cols, "z")
    image, sums = pl.pallas_call(
        image_kernel,
        in_specs=[VMEM] * 3,
        out_specs=[VMEM] * 2,
        out_shape=[f32(OBJ, WIDTH), f32(devices, 128)],
        compiler_params=params(4),
    )(by_rows, by_cols, kept)
    sums = exchanged(sums.reshape(devices, 1, 128), AXES).reshape(devices, 128)
    return pl.pallas_call(
        update_kernel,
        in_specs=[VMEM] * 3,
        out_specs=[VMEM] * 3,
        out_shape=[f32(OBJ, WIDTH)] * 3,
        compiler_params=params(4),
    )(sums, kept, image)


def solution(mesh):
    own = Mesh(mesh.devices.reshape(SIZES), AXES)
    split = P(None, AXES)
    return jax.shard_map(
        shards,
        mesh=own,
        in_specs=(split, split, split, split, P(), P()),
        out_specs=(split, split, split),
        check_vma=False,
    )
```

profile of v0, /device:TPU:1, one launch (start us, length us, event | category | flops | bytes accessed | tf_op | source)
XLA Modules:
  0.0 116.2 jit_solution(16376356387764859029)
XLA Ops:
  0.6 1.6 %shard_map.85 = (bf16[8,48,384]{2,1,0:T(8,128)(2,1)}, bf16[1,48,384]{2,1,0:T(8,128)(2,1)}, f32[5,4,384]{2,1,0:T(4,128)}) custom-call(bf16[32,384]{1,0:T(8,128)(2,1)} %points.1, f32[4,384]{1,0:T(4,128)} %direction.1, f32[4,384]{1,0:T(4,128)} %residual.1, f32[4,384]{1,0:T(4,128)} %solution.1, f32[4]{0:T(128)} %outscale.1, f32[4]{0:T(128)} %noise.1), custom_call_target="tpu_custom_call" | custom-call | tf_op jit(solution)/shard_map/pallas_call | solution.py:291
  2.2 0.0 copy-start.1
  2.2 9.1 %all-to-all-start = ((bf16[8,48,384]{2,1,0:T(8,128)(2,1)}), bf16[8,48,384]{2,1,0:T(8,128)(2,1)S(1)}, u32[]{:S(2)}, u32[]{:S(2)}) async-start(bf16[8,48,384]{2,1,0:T(8,128)(2,1)} %get-tuple-element.17), calls=%async_computation | async-start | bytes 589824 | tf_op jit(solution)/shard_map/all_to_all | solution.py:280
  11.4 0.0 copy-done.1
  11.4 1.0 collective-permute-start
  12.4 0.9 collective-permute-done
  13.3 1.3 %collective-permute-start.1 = (bf16[2,48,384]{2,1,0:T(8,128)(2,1)S(1)}, bf16[2,48,384]{2,1,0:T(8,128)(2,1)S(1)}, u32[]{:S(2)}, u32[]{:S(2)}) collective-permute-start(bf16[2,48,384]{2,1,0:T(8,128)(2,1)S(1)} %constant_dynamic-update-slice_fusion.r0), channel_id=1, source_target_pairs={{0,64},{64,128},{128,192},{192,0},{1,65},{65,129},{129,193},{193,1... | collective-permute-start | bytes 221192 | tf_op jit(solution)/shard_map/ppermute | solution.py:285
  14.6 2.6 %collective-permute-start.2 = (bf16[2,48,384]{2,1,0:T(8,128)(2,1)S(1)}, bf16[2,48,384]{2,1,0:T(8,128)(2,1)S(1)}, u32[]{:S(2)}, u32[]{:S(2)}) collective-permute-start(bf16[2,48,384]{2,1,0:T(8,128)(2,1)S(1)} %constant_dynamic-update-slice_fusion.r0), channel_id=1, source_target_pairs={{0,128},{64,192},{128,0},{192,64},{1,129},{65,193},{129,1},{193,65... | collective-permute-start | bytes 221192 | tf_op jit(solution)/shard_map/ppermute | solution.py:285
  17.2 1.1 collective-permute-start.3
  18.3 0.1 pad_add_fusion.place
  18.4 4.1 %all-to-all-done.cols = bf16[8,48,384]{2,1,0:T(8,128)(2,1)S(1)} async-done(((bf16[8,48,384]{2,1,0:T(8,128)(2,1)}), bf16[8,48,384]{2,1,0:T(8,128)(2,1)S(1)}, u32[]{:S(2)}, u32[]{:S(2)}) %all-to-all-start) | async-done | bytes 294944 | tf_op jit(solution)/shard_map/all_to_all | solution.py:280
  22.5 2.5 %collective-permute-start.4 = (bf16[8,48,384]{2,1,0:T(8,128)(2,1)S(1)}, bf16[8,48,384]{2,1,0:T(8,128)(2,1)S(1)}, u32[]{:S(2)}, u32[]{:S(2)}) collective-permute-start(bf16[8,48,384]{2,1,0:T(8,128)(2,1)S(1)} %all-to-all-done.cols), channel_id=1, source_target_pairs={{0,48},{16,0},{32,16},{48,32},{1,49},{17,1},{33,17},{49,33},{2,50}... | collective-permute-start | bytes 884744 | tf_op jit(solution)/shard_map/ppermute | solution.py:285
  25.0 0.5 collective-permute-start.5
  25.5 0.0 collective-permute-done.1.r1
  25.5 0.0 collective-permute-done.2.r2
  25.5 0.0 collective-permute-done.3.r3
  25.5 12.6 %shard_map.86 = (bf16[128,3072]{1,0:T(8,128)(2,1)S(1)}, bf16[16,4608]{1,0:T(8,128)(2,1)S(1)}, f8e4m3fn[16,4608]{1,0:T(8,128)(4,1)S(1)}, f32[16,3072]{1,0:T(8,128)S(1)}, f32[8,4,384]{2,1,0:T(4,128)S(1)}) custom-call(s32[4]{0:T(128)S(1)} %pad_add_fusion.place, bf16[2,48,384]{2,1,0:T(8,128)(2,1)S(1)} %constant_dynamic-update-slice_fusion.r0, ...), custom_call_target="tpu_custom_call" | custom-call | flops 8000000000 | bytes 1000000 | tf_op jit(solution)/shard_map/pallas_call | solution.py:301
  38.2 0.0 collective-permute-done.4.cols1
  38.2 0.0 collective-permute-done.5.cols2
  38.2 32.9 %shard_map.87 = (f32[8,4,384]{2,1,0:T(4,128)}, f32[8,4,384]{2,1,0:T(4,128)S(1)}, f32[8,4,384]{2,1,0:T(4,128)S(1)}) custom-call(s32[4]{0:T(128)S(1)} %pad_add_fusion.place, bf16[128,3072]{1,0:T(8,128)(2,1)S(1)} %get-tuple-element.18.ax, bf16[16,4608]{1,0:T(8,128)(2,1)S(1)} %get-tuple-element.19.dr, f8e4m3fn[16,4608]{1,0:T(8,128)(4,1)S(1)} %get-tuple-element.20.dr8, ...), custom_call_target="tpu_custom_call" | custom-call | flops 24000000000 | bytes 1000000 | tf_op jit(solution)/shard_map/pallas_call | solution.py:324
  71.1 0.6 collective-permute-start.6
  71.7 1.9 %collective-permute-start.7 = (f32[8,4,384]{2,1,0:T(4,128)S(1)}, f32[8,4,384]{2,1,0:T(4,128)S(1)}, u32[]{:S(2)}, u32[]{:S(2)}) collective-permute-start(f32[8,4,384]{2,1,0:T(4,128)S(1)} %get-tuple-element.25), channel_id=1, source_target_pairs={{0,32},{16,48},{32,0},{48,16},{1,33},{17,49},{33,1},{49,17},{2,34}... | collective-permute-start | bytes 147464 | tf_op jit(solution)/shard_map/ppermute | solution.py:285
  73.5 7.7 %all-to-all-start.1 = ((f32[8,4,384]{2,1,0:T(4,128)}), f32[8,4,384]{2,1,0:T(4,128)S(1)}, u32[]{:S(2)}, u32[]{:S(2)}) async-start(f32[8,4,384]{2,1,0:T(4,128)} %get-tuple-element.22), calls=%async_computation.1 | async-start | bytes 98304 | tf_op jit(solution)/shard_map/all_to_all | solution.py:280
  81.2 0.0 collective-permute-done.6.one
  81.2 0.0 collective-permute-done.7.two
  81.2 0.0 copy-start
  81.3 4.7 %all-to-all-done.1.by_rows = f32[8,4,384]{2,1,0:T(4,128)S(1)} async-done(((f32[8,4,384]{2,1,0:T(4,128)}), f32[8,4,384]{2,1,0:T(4,128)S(1)}, u32[]{:S(2)}, u32[]{:S(2)}) %all-to-all-start.1) | async-done | bytes 49184 | tf_op jit(solution)/shard_map/all_to_all | solution.py:280
  86.0 9.5 %all_to_all.20.by_cols = f32[8,4,384]{2,1,0:T(4,128)S(1)} all-to-all(f32[8,4,384]{2,1,0:T(4,128)S(1)} %shard_map.88), channel_id=1, replica_groups=mesh['y'=4,'x'=4,'core'=2,'z'=8] {'z'}, dimensions={0} | all-to-all | bytes 98304 | tf_op jit(solution)/shard_map/all_to_all | solution.py:280
  95.5 0.0 copy-done
  95.5 0.1 shard_map.89
  95.6 19.8 %all_to_all.21 = f32[256,1,128]{2,1,0:T(1,128)S(1)} all-to-all(f32[256,1,128]{2,1,0:T(1,128)S(1)} %bitcast.9), channel_id=1, replica_groups=mesh['y'=4,'x'=4,'core'=2,'z'=8] {'y','x','core','z'}, dimensions={0} | all-to-all | bytes 262144 | tf_op jit(solution)/shard_map/all_to_all | solution.py:280
  115.4 0.7 shard_map.90
  (3 shorter events, 0.0 us)
Async XLA Ops:
  2.2 9.2 %copy-start.1 = (bf16[1,48,384]{2,1,0:T(8,128)(2,1)S(1)}, bf16[1,48,384]{2,1,0:T(8,128)(2,1)}, u32[]{:S(2)}) copy-start(bf16[1,48,384]{2,1,0:T(8,128)(2,1)} %get-tuple-element.16) | copy-start | bytes 110596
  2.2 20.3 %all-to-all-start = ((bf16[8,48,384]{2,1,0:T(8,128)(2,1)}), bf16[8,48,384]{2,1,0:T(8,128)(2,1)S(1)}, u32[]{:S(2)}, u32[]{:S(2)}) async-start(bf16[8,48,384]{2,1,0:T(8,128)(2,1)} %get-tuple-element.17), calls=%async_computation | async-start | bytes 589824 | tf_op jit(solution)/shard_map/all_to_all | solution.py:280
  11.4 1.9 %collective-permute-start = (bf16[1,48,384]{2,1,0:T(8,128)(2,1)S(1)}, bf16[1,48,384]{2,1,0:T(8,128)(2,1)S(1)}, u32[]{:S(2)}, u32[]{:S(2)}) collective-permute-start(bf16[1,48,384]{2,1,0:T(8,128)(2,1)S(1)} %copy-done.1), channel_id=1, source_target_pairs={{0,8},{8,0},{1,9},{9,1},{2,10},{10,2},{3,11},{11,3},{4,12},{12,4},... | collective-permute-start | bytes 110600 | tf_op jit(solution)/shard_map/ppermute | solution.py:285
  13.3 12.2 %collective-permute-start.1 = (bf16[2,48,384]{2,1,0:T(8,128)(2,1)S(1)}, bf16[2,48,384]{2,1,0:T(8,128)(2,1)S(1)}, u32[]{:S(2)}, u32[]{:S(2)}) collective-permute-start(bf16[2,48,384]{2,1,0:T(8,128)(2,1)S(1)} %constant_dynamic-update-slice_fusion.r0), channel_id=1, source_target_pairs={{0,64},{64,128},{128,192},{192,0},{1,65},{65,129},{129,193},{193,1... | collective-permute-start | bytes 221192 | tf_op jit(solution)/shard_map/ppermute | solution.py:285
  14.6 10.9 %collective-permute-start.2 = (bf16[2,48,384]{2,1,0:T(8,128)(2,1)S(1)}, bf16[2,48,384]{2,1,0:T(8,128)(2,1)S(1)}, u32[]{:S(2)}, u32[]{:S(2)}) collective-permute-start(bf16[2,48,384]{2,1,0:T(8,128)(2,1)S(1)} %constant_dynamic-update-slice_fusion.r0), channel_id=1, source_target_pairs={{0,128},{64,192},{128,0},{192,64},{1,129},{65,193},{129,1},{193,65... | collective-permute-start | bytes 221192 | tf_op jit(solution)/shard_map/ppermute | solution.py:285
  17.2 8.3 %collective-permute-start.3 = (bf16[2,48,384]{2,1,0:T(8,128)(2,1)S(1)}, bf16[2,48,384]{2,1,0:T(8,128)(2,1)S(1)}, u32[]{:S(2)}, u32[]{:S(2)}) collective-permute-start(bf16[2,48,384]{2,1,0:T(8,128)(2,1)S(1)} %constant_dynamic-update-slice_fusion.r0), channel_id=1, source_target_pairs={{0,192},{64,0},{128,64},{192,128},{1,193},{65,1},{129,65},{193,129... | collective-permute-start | bytes 221192 | tf_op jit(solution)/shard_map/ppermute | solution.py:285
  22.5 15.7 %collective-permute-start.4 = (bf16[8,48,384]{2,1,0:T(8,128)(2,1)S(1)}, bf16[8,48,384]{2,1,0:T(8,128)(2,1)S(1)}, u32[]{:S(2)}, u32[]{:S(2)}) collective-permute-start(bf16[8,48,384]{2,1,0:T(8,128)(2,1)S(1)} %all-to-all-done.cols), channel_id=1, source_target_pairs={{0,48},{16,0},{32,16},{48,32},{1,49},{17,1},{33,17},{49,33},{2,50}... | collective-permute-start | bytes 884744 | tf_op jit(solution)/shard_map/ppermute | solution.py:285
  25.0 13.2 %collective-permute-start.5 = (bf16[8,48,384]{2,1,0:T(8,128)(2,1)S(1)}, bf16[8,48,384]{2,1,0:T(8,128)(2,1)S(1)}, u32[]{:S(2)}, u32[]{:S(2)}) collective-permute-start(bf16[8,48,384]{2,1,0:T(8,128)(2,1)S(1)} %all-to-all-done.cols), channel_id=1, source_target_pairs={{0,32},{16,48},{32,0},{48,16},{1,33},{17,49},{33,1},{49,17},{2,34}... | collective-permute-start | bytes 884744 | tf_op jit(solution)/shard_map/ppermute | solution.py:285
  71.1 10.1 %collective-permute-start.6 = (f32[8,4,384]{2,1,0:T(4,128)S(1)}, f32[8,4,384]{2,1,0:T(4,128)S(1)}, u32[]{:S(2)}, u32[]{:S(2)}) collective-permute-start(f32[8,4,384]{2,1,0:T(4,128)S(1)} %get-tuple-element.24), channel_id=1, source_target_pairs={{0,16},{16,32},{32,48},{48,0},{1,17},{17,33},{33,49},{49,1},{2,18}... | collective-permute-start | bytes 147464 | tf_op jit(solution)/shard_map/ppermute | solution.py:285
  71.7 9.5 %collective-permute-start.7 = (f32[8,4,384]{2,1,0:T(4,128)S(1)}, f32[8,4,384]{2,1,0:T(4,128)S(1)}, u32[]{:S(2)}, u32[]{:S(2)}) collective-permute-start(f32[8,4,384]{2,1,0:T(4,128)S(1)} %get-tuple-element.25), channel_id=1, source_target_pairs={{0,32},{16,48},{32,0},{48,16},{1,33},{17,49},{33,1},{49,17},{2,34}... | collective-permute-start | bytes 147464 | tf_op jit(solution)/shard_map/ppermute | solution.py:285
  73.5 12.4 %all-to-all-start.1 = ((f32[8,4,384]{2,1,0:T(4,128)}), f32[8,4,384]{2,1,0:T(4,128)S(1)}, u32[]{:S(2)}, u32[]{:S(2)}) async-start(f32[8,4,384]{2,1,0:T(4,128)} %get-tuple-element.22), calls=%async_computation.1 | async-start | bytes 98304 | tf_op jit(solution)/shard_map/all_to_all | solution.py:280
  81.2 14.3 %copy-start = (f32[5,4,384]{2,1,0:T(4,128)S(1)}, f32[5,4,384]{2,1,0:T(4,128)}, u32[]{:S(2)}) copy-start(f32[5,4,384]{2,1,0:T(4,128)} %get-tuple-element.26.kept) | copy-start | bytes 92164
where the time goes:
time: 117 us; the launch traced here: 116 us
  Pallas kernels  48 us (41%)
  blocking collectives  29.3 us (25%)
  starting transfers between devices  28.3 us (24%)
  waiting for transfers between devices  9.78 us (8%)
    pallas_call x1, Pallas kernels, shards(): pl.pallas_call(far_kernel, in_specs=[SMEM] + [VMEM] * 6, out_specs=[VMEM]...  32.9 us
    all_to_all x2, blocking collectives, exchanged(): return lax.all_to_all(x, axis, 0, 0)  29.3 us
    all_to_all x2, starting transfers between devices, exchanged(): return lax.all_to_all(x, axis, 0, 0)  16.8 us
    pallas_call x1, Pallas kernels, shards(): pl.pallas_call(near_kernel, in_specs=[SMEM] + [VMEM] * 5, out_specs=[VMEM...  12.6 us
    ppermute x8, starting transfers between devices, from_ahead(): lax.ppermute(x, axis, [(i, (i - by) % length) for i in range(length)])  11.5 us
    all_to_all x2, waiting for transfers between devices, exchanged(): return lax.all_to_all(x, axis, 0, 0)  8.89 us
  transfers between devices with their start and end apart: 10, of which 3 were waited for; matrix products, arithmetic and copies ran while one was open for 0% of the time, Pallas kernels for 11%

commit v1 on v0

--- a/solution.py
+++ b/solution.py
@@ -76,7 +76,11 @@
 
 
 def both(a, hi, lo, dims=((1,), (0,))):
-    return dot(a[0], hi, dims) + (1.0 / LOW) * dot(a[1], lo, dims)
+    return dot(a[0], hi, dims)[: 2 * OBJ], dot(a[1], lo, dims)[: 2 * OBJ]
+
+
+def joined(high, low):
+    return high + (1.0 / LOW) * low
 
 
 def fine(tail):
@@ -107,7 +111,7 @@
     def by_row(step, hi, lo, o, first):
         i, at, _ = place_of(step)
         lanes = pl.ds(pl.multiple_of(jnp.where(first, LANES, at) + o, 128), STRIP)
-        row_acc[:, lanes] += both((dc[i], dc8[i]), hi[:, o : o + STRIP], lo[:, o : o + STRIP])
+        row_acc[:, lanes] += joined(*both((dc[i], dc8[i]), hi[:, o : o + STRIP], lo[:, o : o + STRIP]))
 
     def half(step, x, x_next, hi, lo, hi_last, lo_last):
         last, following = jnp.maximum(step - 1, 0), jnp.minimum(step + 1, count - 1)
@@ -115,11 +119,11 @@
         for o in range(0, HALF, STRIP):
             distances(following, x_next, o)
             part = by_col(last, hi_last, lo_last, o)
-            total = part if total is None else total + part
+            total = part if total is None else (total[0] + part[0], total[1] + part[1])
             by_row(last, hi_last, lo_last, o, step == 0)
             got = weights(x[:, o : o + STRIP])
             hi[:, o : o + STRIP], lo[:, o : o + STRIP] = got
-        col_acc[jnp.where(step == 0, spare, place_of(last)[0])] += total
+        col_acc[jnp.where(step == 0, spare, place_of(last)[0])] += joined(*total)
 
     for o in range(0, HALF, STRIP):
         distances(0, xa, o)
@@ -132,9 +136,9 @@
     total = None
     for o in range(0, HALF, STRIP):
         part = by_col(count - 1, hb, lb, o)
-        total = part if total is None else total + part
+        total = part if total is None else (total[0] + part[0], total[1] + part[1])
         by_row(count - 1, hb, lb, o, False)
-    col_acc[place_of(count - 1)[0]] += total
+    col_acc[place_of(count - 1)[0]] += joined(*total)
 
 
 def stages():
@@ -201,7 +205,7 @@
 
     lanes = pl.ds(HALF, WIDTH)
     hi, lo = weights(dot(bt[0], ax[:, lanes]))
-    row_acc[:, lanes] += both((dc[0], dc8[0]), hi, lo)
+    row_acc[:, lanes] += joined(*both((dc[0], dc8[0]), hi, lo))
     row_out[...] = row_acc[:, :LANES]
     for i in range(BLOCKS):
         got = folded(col_acc[i]) if i < 5 else jnp.zeros((OBJ, WIDTH), jnp.float32)
@@ -306,16 +310,16 @@
             bf16(DEPTH, LANES),
             bf16(16, LANES + HALF),
             jax.ShapeDtypeStruct((16, LANES + HALF), FINE),
-            f32(16, LANES),
+            f32(2 * OBJ, LANES),
             f32(BLOCKS, OBJ, WIDTH),
         ],
         scratch_shapes=[
-            pltpu.VMEM((16, LANES + HALF), jnp.float32),
+            pltpu.VMEM((2 * OBJ, LANES + HALF), jnp.float32),
             pltpu.VMEM((BLOCKS, PACK, WIDTH), jnp.bfloat16),
             pltpu.VMEM((5, WIDTH, DEPTH), jnp.bfloat16),
             pltpu.VMEM((5, 16, WIDTH), jnp.bfloat16),
             pltpu.VMEM((5, 16, WIDTH), FINE),
-            pltpu.VMEM((6, 16, WIDTH), jnp.float32),
+            pltpu.VMEM((6, 2 * OBJ, WIDTH), jnp.float32),
         ]
         + stages(),
         compiler_params=params(),
@@ -327,11 +331,11 @@
         out_specs=[VMEM] * 3,
         out_shape=[f32(BLOCKS, OBJ, WIDTH)] * 3,
         scratch_shapes=[
-            pltpu.VMEM((16, LANES + HALF), jnp.float32),
+            pltpu.VMEM((2 * OBJ, LANES + HALF), jnp.float32),
             pltpu.VMEM((12, WIDTH, DEPTH), jnp.bfloat16),
             pltpu.VMEM((12, 16, WIDTH), jnp.bfloat16),
             pltpu.VMEM((12, 16, WIDTH), FINE),
-            pltpu.VMEM((13, 16, WIDTH), jnp.float32),
+            pltpu.VMEM((13, 2 * OBJ, WIDTH), jnp.float32),
         ]
         + stages(),
         compiler_params=params(),

time: 117 us -> 116 us (level)
  no operation moved by 1% of the time
where the time goes in v1:
time: 116 us
  Pallas kernels  47.1 us (41%)
  blocking collectives  29.5 us (25%)
  starting transfers between devices  28.4 us (24%)
  waiting for transfers between devices  9.77 us (8%)
    pallas_call x1, Pallas kernels, shards(): pl.pallas_call(far_kernel, in_specs=[SMEM] + [VMEM] * 6, out_specs=[VMEM]...  32.3 us
    all_to_all x2, blocking collectives, exchanged(): return lax.all_to_all(x, axis, 0, 0)  29.5 us
    all_to_all x2, starting transfers between devices, exchanged(): return lax.all_to_all(x, axis, 0, 0)  16.9 us
    pallas_call x1, Pallas kernels, shards(): pl.pallas_call(near_kernel, in_specs=[SMEM] + [VMEM] * 5, out_specs=[VMEM...  12.4 us
    ppermute x8, starting transfers between devices, from_ahead(): lax.ppermute(x, axis, [(i, (i - by) % length) for i in range(length)])  11.5 us
    all_to_all x2, waiting for transfers between devices, exchanged(): return lax.all_to_all(x, axis, 0, 0)  8.89 us
  transfers between devices with their start and end apart: 10, of which 3 were waited for; matrix products, arithmetic and copies ran while one was open for 0% of the time, Pallas kernels for 11%

profile of v1, /device:TPU:1, one launch (start us, length us, event | category | flops | bytes accessed | tf_op | source)
XLA Modules:
  0.0 115.6 jit_solution(5990319725249529926)
XLA Ops:
  0.6 1.6 %shard_map.85 = (bf16[8,48,384]{2,1,0:T(8,128)(2,1)}, bf16[1,48,384]{2,1,0:T(8,128)(2,1)}, f32[5,4,384]{2,1,0:T(4,128)}) custom-call(bf16[32,384]{1,0:T(8,128)(2,1)} %points.1, f32[4,384]{1,0:T(4,128)} %direction.1, f32[4,384]{1,0:T(4,128)} %residual.1, f32[4,384]{1,0:T(4,128)} %solution.1, f32[4]{0:T(128)} %outscale.1, f32[4]{0:T(128)} %noise.1), custom_call_target="tpu_custom_call" | custom-call | tf_op jit(solution)/shard_map/pallas_call | solution.py:295
  2.2 0.0 copy-start.1
  2.2 9.1 %all-to-all-start = ((bf16[8,48,384]{2,1,0:T(8,128)(2,1)}), bf16[8,48,384]{2,1,0:T(8,128)(2,1)S(1)}, u32[]{:S(2)}, u32[]{:S(2)}) async-start(bf16[8,48,384]{2,1,0:T(8,128)(2,1)} %get-tuple-element.17), calls=%async_computation | async-start | bytes 589824 | tf_op jit(solution)/shard_map/all_to_all | solution.py:284
  11.4 0.0 copy-done.1
  11.4 1.0 collective-permute-start
  12.4 0.9 collective-permute-done
  13.3 1.3 %collective-permute-start.1 = (bf16[2,48,384]{2,1,0:T(8,128)(2,1)S(1)}, bf16[2,48,384]{2,1,0:T(8,128)(2,1)S(1)}, u32[]{:S(2)}, u32[]{:S(2)}) collective-permute-start(bf16[2,48,384]{2,1,0:T(8,128)(2,1)S(1)} %constant_dynamic-update-slice_fusion.r0), channel_id=1, source_target_pairs={{0,64},{64,128},{128,192},{192,0},{1,65},{65,129},{129,193},{193,1... | collective-permute-start | bytes 221192 | tf_op jit(solution)/shard_map/ppermute | solution.py:289
  14.6 2.6 %collective-permute-start.2 = (bf16[2,48,384]{2,1,0:T(8,128)(2,1)S(1)}, bf16[2,48,384]{2,1,0:T(8,128)(2,1)S(1)}, u32[]{:S(2)}, u32[]{:S(2)}) collective-permute-start(bf16[2,48,384]{2,1,0:T(8,128)(2,1)S(1)} %constant_dynamic-update-slice_fusion.r0), channel_id=1, source_target_pairs={{0,128},{64,192},{128,0},{192,64},{1,129},{65,193},{129,1},{193,65... | collective-permute-start | bytes 221192 | tf_op jit(solution)/shard_map/ppermute | solution.py:289
  17.2 1.1 collective-permute-start.3
  18.3 0.1 pad_add_fusion.place
  18.4 4.1 %all-to-all-done.cols = bf16[8,48,384]{2,1,0:T(8,128)(2,1)S(1)} async-done(((bf16[8,48,384]{2,1,0:T(8,128)(2,1)}), bf16[8,48,384]{2,1,0:T(8,128)(2,1)S(1)}, u32[]{:S(2)}, u32[]{:S(2)}) %all-to-all-start) | async-done | bytes 294944 | tf_op jit(solution)/shard_map/all_to_all | solution.py:284
  22.5 2.5 %collective-permute-start.4 = (bf16[8,48,384]{2,1,0:T(8,128)(2,1)S(1)}, bf16[8,48,384]{2,1,0:T(8,128)(2,1)S(1)}, u32[]{:S(2)}, u32[]{:S(2)}) collective-permute-start(bf16[8,48,384]{2,1,0:T(8,128)(2,1)S(1)} %all-to-all-done.cols), channel_id=1, source_target_pairs={{0,48},{16,0},{32,16},{48,32},{1,49},{17,1},{33,17},{49,33},{2,50}... | collective-permute-start | bytes 884744 | tf_op jit(solution)/shard_map/ppermute | solution.py:289
  25.0 0.5 collective-permute-start.5
  25.5 0.0 collective-permute-done.1.r1
  25.5 0.0 collective-permute-done.2.r2
  25.5 0.0 collective-permute-done.3.r3
  25.5 12.4 %shard_map.86 = (bf16[128,3072]{1,0:T(8,128)(2,1)S(1)}, bf16[16,4608]{1,0:T(8,128)(2,1)S(1)}, f8e4m3fn[16,4608]{1,0:T(8,128)(4,1)S(1)}, f32[8,3072]{1,0:T(8,128)S(1)}, f32[8,4,384]{2,1,0:T(4,128)S(1)}) custom-call(s32[4]{0:T(128)S(1)} %pad_add_fusion.place, bf16[2,48,384]{2,1,0:T(8,128)(2,1)S(1)} %constant_dynamic-update-slice_fusion.r0, ...), custom_call_target="tpu_custom_call" | custom-call | flops 8000000000 | bytes 1000000 | tf_op jit(solution)/shard_map/pallas_call | solution.py:305
  37.9 0.0 collective-permute-done.4.cols1
  37.9 0.0 collective-permute-done.5.cols2
  38.0 32.3 %shard_map.87 = (f32[8,4,384]{2,1,0:T(4,128)}, f32[8,4,384]{2,1,0:T(4,128)S(1)}, f32[8,4,384]{2,1,0:T(4,128)S(1)}) custom-call(s32[4]{0:T(128)S(1)} %pad_add_fusion.place, bf16[128,3072]{1,0:T(8,128)(2,1)S(1)} %get-tuple-element.18.ax, bf16[16,4608]{1,0:T(8,128)(2,1)S(1)} %get-tuple-element.19.dr, f8e4m3fn[16,4608]{1,0:T(8,128)(4,1)S(1)} %get-tuple-element.20.dr8, ...), custom_call_target="tpu_custom_call" | custom-call | flops 24000000000 | bytes 1000000 | tf_op jit(solution)/shard_map/pallas_call | solution.py:328
  70.3 0.6 collective-permute-start.6
  70.9 1.8 %collective-permute-start.7 = (f32[8,4,384]{2,1,0:T(4,128)S(1)}, f32[8,4,384]{2,1,0:T(4,128)S(1)}, u32[]{:S(2)}, u32[]{:S(2)}) collective-permute-start(f32[8,4,384]{2,1,0:T(4,128)S(1)} %get-tuple-element.25), channel_id=1, source_target_pairs={{0,32},{16,48},{32,0},{48,16},{1,33},{17,49},{33,1},{49,17},{2,34}... | collective-permute-start | bytes 147464 | tf_op jit(solution)/shard_map/ppermute | solution.py:289
  72.7 7.8 %all-to-all-start.1 = ((f32[8,4,384]{2,1,0:T(4,128)}), f32[8,4,384]{2,1,0:T(4,128)S(1)}, u32[]{:S(2)}, u32[]{:S(2)}) async-start(f32[8,4,384]{2,1,0:T(4,128)} %get-tuple-element.22), calls=%async_computation.1 | async-start | bytes 98304 | tf_op jit(solution)/shard_map/all_to_all | solution.py:284
  80.5 0.0 collective-permute-done.6.one
  80.5 0.0 collective-permute-done.7.two
  80.5 0.0 copy-start
  80.5 4.7 %all-to-all-done.1.by_rows = f32[8,4,384]{2,1,0:T(4,128)S(1)} async-done(((f32[8,4,384]{2,1,0:T(4,128)}), f32[8,4,384]{2,1,0:T(4,128)S(1)}, u32[]{:S(2)}, u32[]{:S(2)}) %all-to-all-start.1) | async-done | bytes 49184 | tf_op jit(solution)/shard_map/all_to_all | solution.py:284
  85.3 9.4 %all_to_all.20.by_cols = f32[8,4,384]{2,1,0:T(4,128)S(1)} all-to-all(f32[8,4,384]{2,1,0:T(4,128)S(1)} %shard_map.88), channel_id=1, replica_groups=mesh['y'=4,'x'=4,'core'=2,'z'=8] {'z'}, dimensions={0} | all-to-all | bytes 98304 | tf_op jit(solution)/shard_map/all_to_all | solution.py:284
  94.7 0.0 copy-done
  94.7 0.1 shard_map.89
  94.8 20.1 %all_to_all.21 = f32[256,1,128]{2,1,0:T(1,128)S(1)} all-to-all(f32[256,1,128]{2,1,0:T(1,128)S(1)} %bitcast.9), channel_id=1, replica_groups=mesh['y'=4,'x'=4,'core'=2,'z'=8] {'y','x','core','z'}, dimensions={0} | all-to-all | bytes 262144 | tf_op jit(solution)/shard_map/all_to_all | solution.py:284
  114.9 0.7 shard_map.90
  (3 shorter events, 0.0 us)
Async XLA Ops:
  2.2 9.2 %copy-start.1 = (bf16[1,48,384]{2,1,0:T(8,128)(2,1)S(1)}, bf16[1,48,384]{2,1,0:T(8,128)(2,1)}, u32[]{:S(2)}) copy-start(bf16[1,48,384]{2,1,0:T(8,128)(2,1)} %get-tuple-element.16) | copy-start | bytes 110596
  2.2 20.3 %all-to-all-start = ((bf16[8,48,384]{2,1,0:T(8,128)(2,1)}), bf16[8,48,384]{2,1,0:T(8,128)(2,1)S(1)}, u32[]{:S(2)}, u32[]{:S(2)}) async-start(bf16[8,48,384]{2,1,0:T(8,128)(2,1)} %get-tuple-element.17), calls=%async_computation | async-start | bytes 589824 | tf_op jit(solution)/shard_map/all_to_all | solution.py:284
  11.4 1.9 %collective-permute-start = (bf16[1,48,384]{2,1,0:T(8,128)(2,1)S(1)}, bf16[1,48,384]{2,1,0:T(8,128)(2,1)S(1)}, u32[]{:S(2)}, u32[]{:S(2)}) collective-permute-start(bf16[1,48,384]{2,1,0:T(8,128)(2,1)S(1)} %copy-done.1), channel_id=1, source_target_pairs={{0,8},{8,0},{1,9},{9,1},{2,10},{10,2},{3,11},{11,3},{4,12},{12,4},... | collective-permute-start | bytes 110600 | tf_op jit(solution)/shard_map/ppermute | solution.py:289
  13.3 12.2 %collective-permute-start.1 = (bf16[2,48,384]{2,1,0:T(8,128)(2,1)S(1)}, bf16[2,48,384]{2,1,0:T(8,128)(2,1)S(1)}, u32[]{:S(2)}, u32[]{:S(2)}) collective-permute-start(bf16[2,48,384]{2,1,0:T(8,128)(2,1)S(1)} %constant_dynamic-update-slice_fusion.r0), channel_id=1, source_target_pairs={{0,64},{64,128},{128,192},{192,0},{1,65},{65,129},{129,193},{193,1... | collective-permute-start | bytes 221192 | tf_op jit(solution)/shard_map/ppermute | solution.py:289
  14.6 10.9 %collective-permute-start.2 = (bf16[2,48,384]{2,1,0:T(8,128)(2,1)S(1)}, bf16[2,48,384]{2,1,0:T(8,128)(2,1)S(1)}, u32[]{:S(2)}, u32[]{:S(2)}) collective-permute-start(bf16[2,48,384]{2,1,0:T(8,128)(2,1)S(1)} %constant_dynamic-update-slice_fusion.r0), channel_id=1, source_target_pairs={{0,128},{64,192},{128,0},{192,64},{1,129},{65,193},{129,1},{193,65... | collective-permute-start | bytes 221192 | tf_op jit(solution)/shard_map/ppermute | solution.py:289
  17.2 8.3 %collective-permute-start.3 = (bf16[2,48,384]{2,1,0:T(8,128)(2,1)S(1)}, bf16[2,48,384]{2,1,0:T(8,128)(2,1)S(1)}, u32[]{:S(2)}, u32[]{:S(2)}) collective-permute-start(bf16[2,48,384]{2,1,0:T(8,128)(2,1)S(1)} %constant_dynamic-update-slice_fusion.r0), channel_id=1, source_target_pairs={{0,192},{64,0},{128,64},{192,128},{1,193},{65,1},{129,65},{193,129... | collective-permute-start | bytes 221192 | tf_op jit(solution)/shard_map/ppermute | solution.py:289
  22.5 15.4 %collective-permute-start.4 = (bf16[8,48,384]{2,1,0:T(8,128)(2,1)S(1)}, bf16[8,48,384]{2,1,0:T(8,128)(2,1)S(1)}, u32[]{:S(2)}, u32[]{:S(2)}) collective-permute-start(bf16[8,48,384]{2,1,0:T(8,128)(2,1)S(1)} %all-to-all-done.cols), channel_id=1, source_target_pairs={{0,48},{16,0},{32,16},{48,32},{1,49},{17,1},{33,17},{49,33},{2,50}... | collective-permute-start | bytes 884744 | tf_op jit(solution)/shard_map/ppermute | solution.py:289
  25.0 12.9 %collective-permute-start.5 = (bf16[8,48,384]{2,1,0:T(8,128)(2,1)S(1)}, bf16[8,48,384]{2,1,0:T(8,128)(2,1)S(1)}, u32[]{:S(2)}, u32[]{:S(2)}) collective-permute-start(bf16[8,48,384]{2,1,0:T(8,128)(2,1)S(1)} %all-to-all-done.cols), channel_id=1, source_target_pairs={{0,32},{16,48},{32,0},{48,16},{1,33},{17,49},{33,1},{49,17},{2,34}... | collective-permute-start | bytes 884744 | tf_op jit(solution)/shard_map/ppermute | solution.py:289
  70.3 10.2 %collective-permute-start.6 = (f32[8,4,384]{2,1,0:T(4,128)S(1)}, f32[8,4,384]{2,1,0:T(4,128)S(1)}, u32[]{:S(2)}, u32[]{:S(2)}) collective-permute-start(f32[8,4,384]{2,1,0:T(4,128)S(1)} %get-tuple-element.24), channel_id=1, source_target_pairs={{0,16},{16,32},{32,48},{48,0},{1,17},{17,33},{33,49},{49,1},{2,18}... | collective-permute-start | bytes 147464 | tf_op jit(solution)/shard_map/ppermute | solution.py:289
  70.9 9.6 %collective-permute-start.7 = (f32[8,4,384]{2,1,0:T(4,128)S(1)}, f32[8,4,384]{2,1,0:T(4,128)S(1)}, u32[]{:S(2)}, u32[]{:S(2)}) collective-permute-start(f32[8,4,384]{2,1,0:T(4,128)S(1)} %get-tuple-element.25), channel_id=1, source_target_pairs={{0,32},{16,48},{32,0},{48,16},{1,33},{17,49},{33,1},{49,17},{2,34}... | collective-permute-start | bytes 147464 | tf_op jit(solution)/shard_map/ppermute | solution.py:289
  72.7 12.6 %all-to-all-start.1 = ((f32[8,4,384]{2,1,0:T(4,128)}), f32[8,4,384]{2,1,0:T(4,128)S(1)}, u32[]{:S(2)}, u32[]{:S(2)}) async-start(f32[8,4,384]{2,1,0:T(4,128)} %get-tuple-element.22), calls=%async_computation.1 | async-start | bytes 98304 | tf_op jit(solution)/shard_map/all_to_all | solution.py:284
  80.5 14.2 %copy-start = (f32[5,4,384]{2,1,0:T(4,128)S(1)}, f32[5,4,384]{2,1,0:T(4,128)}, u32[]{:S(2)}) copy-start(f32[5,4,384]{2,1,0:T(4,128)} %get-tuple-element.26.kept) | copy-start | bytes 92164
